TPU v7x, 32 devices: a whole 2x2x4 slice. The times are simulated.
32 devices in a mesh: row: 4 (over y, x), col: 8 (over z, core).
Axes of the slice: x: 2, y: 2, z: 4, core: 2. Of those that a mesh axis runs over, the one named last changes fastest.
Arguments:
- amplitudes: bfloat16 [10240, 8192], P('row', 'col'), may hold values from -6 to 6
- integrals: bfloat16 [1280, 128, 128], P(('row', 'col')), may hold values from -0.1875 to 0.1875
- tile_ab: int32 [1280], P(('row', 'col')), may hold values from -1 to 19, as said below
- tile_cd: int32 [1280], P(('row', 'col')), may hold values from -1 to 79, as said below
Outputs:
- residual: bfloat16 [10240, 8192], P('row', 'col')
Inputs may be any that keep to these rules, and one draw needn't show every extreme that they name: A slot is live where tile_ab >= 0; then tile_cd >= 0 as well. Empty slots have -1 in both. Each device's live slots come before its empty ones. The live (tile_ab, tile_cd) pairs of one row group are distinct. Each row group holds exactly 145 live slots, and one device of each row group has all its 40 slots live. `tile_cd`: see tile_ab.
All inputs are finite; a program needn't handle non-finite values.
Results may differ from a plain program's by a relative error of at most 0.001.
Values may be sent and summed in bfloat16 or wider, within the bound.
A program may use at most 320 MiB of HBM per device.

v0:
```python
import jax
import jax.numpy as jnp
from jax import lax
from jax.sharding import PartitionSpec as P

TILE = 128
NV = 80


def place_tiles(dense_block, pieces):
    tile_data, ab_code, cd_code = pieces
    ab_index = ab_code.astype(jnp.int32)
    cd_index = cd_code.astype(jnp.int32)
    position = jnp.where(ab_index >= 0, ab_index * NV + cd_index, dense_block.shape[0])
    return dense_block.at[position].add(tile_data, mode="drop")


def body(amplitudes, integrals, tile_ab, tile_cd):
    row_tiles = amplitudes.shape[0] // TILE
    ab_code = tile_ab.astype(jnp.bfloat16)
    cd_code = tile_cd.astype(jnp.bfloat16)
    empty_block = jnp.zeros((row_tiles * NV, TILE, TILE), jnp.bfloat16)
    dense_block = place_tiles(
        empty_block,
        (
            lax.all_gather(integrals, "col", axis=0, tiled=True),
            lax.all_gather(ab_code, "col", axis=0, tiled=True),
            lax.all_gather(cd_code, "col", axis=0, tiled=True),
        ),
    )
    matrix = (
        dense_block.reshape(row_tiles, NV, TILE, TILE)
        .transpose(0, 2, 1, 3)
        .reshape(row_tiles * TILE, NV * TILE)
    )
    result = jnp.dot(
        matrix,
        lax.all_gather(amplitudes, "row", axis=0, tiled=True),
        preferred_element_type=jnp.float32,
    )
    return result.astype(jnp.bfloat16)


def solution(mesh):
    in_specs = (
        P("row", "col"),
        P(("row", "col"), None, None),
        P(("row", "col")),
        P(("row", "col")),
    )
    out_specs = P("row", "col")
    return jax.shard_map(body, mesh=mesh, in_specs=in_specs, out_specs=out_specs, check_vma=False)
```

profile of v0, /device:TPU:0, one launch (start us, length us, event | category | flops | bytes accessed | tf_op | source)
XLA Modules:
  0.0 377.4 jit_solution(17610771200984212118)
XLA Ops:
  6.5 0.0 all-gather.3.cloned.1.call-start
  6.5 0.7 all-gather.3.cloned.1.call-update
  7.3 0.0 all-gather.5.cloned.1.call-start
  7.3 0.7 all-gather.5.cloned.1.call-update
  8.0 0.7 convert_element_type.15
  8.7 0.7 convert_element_type.17
  9.3 1.2 dynamic-slice
  11.2 0.2 dynamic-update-slice
  11.5 0.2 dynamic-update-slice.1
  11.7 18.5 %all-reduce.2 = (bf16[320]{0:T(512)(128)(2,1)S(1)}, bf16[320]{0:T(512)(128)(2,1)S(1)}) all-reduce(bf16[320]{0:T(512)(128)(2,1)S(1)} %dynamic-update-slice, bf16[320]{0:T(512)(128)(2,1)S(1)} %dynamic-update-slice.1), channel_id=1, replica_groups=mesh['row'=4,'col'=8] {'col'}, use_global_device_ids=true, to_apply=%add | all-reduce | flops 640 | bytes 2560
  30.2 81.0 %all-gather.3.cloned.1.call-done = bf16[320,128,128]{2,1,0:T(8,128)(2,1)} async-done(((bf16[40,128,128]{2,1,0:T(8,128)(2,1)}), bf16[320,128,128]{2,1,0:T(8,128)(2,1)}) %all-gather.3.cloned.1.call-update) | async-done | bytes 10485776 | tf_op jit(solution)/shard_map/all_gather | solution.py:26
  111.2 21.7 %broadcast_in_dim.10 = bf16[1600,128,128]{2,1,0:T(8,128)(2,1)} broadcast(bf16[]{:T(256)} %constant.4.clone.1), dimensions={} | broadcast | bytes 52428800 | tf_op jit(solution)/shard_map/broadcast_in_dim | solution.py:22
  132.9 61.8 %scatter_fusion = bf16[1600,128,128]{2,1,0:T(8,128)(2,1)} fusion(bf16[1600,128,128]{2,1,0:T(8,128)(2,1)} %broadcast_in_dim.10, s32[320]{0:T(512)S(1)} %compare_select_fusion, bf16[320,128,128]{2,1,0:T(8,128)(2,1)} %all-gather.3.cloned.1.call-done), kind=kCustom, calls=%fused_computation | custom fusion | flops 5242880 | bytes 31458560 | tf_op jit(solution)/shard_map/scatter-add | solution.py:15
  194.7 53.5 %copy.6 = bf16[20,80,128,128]{3,1,2,0:T(8,128)(2,1)} copy(bf16[20,80,128,128]{3,2,1,0:T(8,128)(2,1)} %bitcast.11) | data formatting | bytes 104857600 | tf_op jit(solution)/shard_map/reshape | solution.py:32
  248.2 56.5 %all-gather.5.cloned.1.call-done = bf16[10240,1024]{1,0:T(8,128)(2,1)} async-done(((bf16[2560,1024]{1,0:T(8,128)(2,1)}), bf16[10240,1024]{1,0:T(8,128)(2,1)}) %all-gather.5.cloned.1.call-update) | async-done | bytes 20971536 | tf_op jit(solution)/shard_map/all_gather | solution.py:38
  304.7 65.9 %fusion.3 = bf16[2560,1024]{1,0:T(8,128)(2,1)} fusion(bf16[10240,1024]{1,0:T(8,128)(2,1)} %all-gather.5.cloned.1.call-done, bf16[320,8,80,128]{3,2,1,0:T(8,128)(2,1)} %bitcast.12), kind=kOutput, calls=%fused_computation.4 | convolution fusion | flops 53689712640 | bytes 78643200 | tf_op jit(solution)/shard_map/dot_general | solution.py:36
  (3 shorter events, 0.0 us)
Async XLA Ops:
  6.5 104.7 %all-gather.3.cloned.1.call-start = ((), (), s32[]{:S(2)}) async-start(), calls=%async_computation | async-start | bytes 11796480 | tf_op jit(solution)/shard_map/all_gather | solution.py:26
  7.3 297.4 %all-gather.5.cloned.1.call-start = ((), (), s32[]{:S(2)}) async-start(), calls=%async_computation.1 | async-start | bytes 26214400 | tf_op jit(solution)/shard_map/all_gather | solution.py:38
Sparse Core Ops, SparseCore 0:
  9.0 102.1 all-gather.2
  113.1 191.5 all-gather.4
where the time goes:
time: 378 us; the launch traced here: 377 us
  waiting for transfers between devices  139 us (37%)
  local copies, waits for them, and re-layouts  76.9 us (20%)
  matrix products  65.9 us (17%)
  other arithmetic  63.1 us (17%)
  blocking collectives  18.5 us (5%)
  between operations  14.1 us (4%)
    all_gather x1, waiting for transfers between devices, body(): lax.all_gather(integrals, 'col', axis=0, tiled=True)  81 us
    dot_general x1, matrix products, body(): jnp.dot(matrix, lax.all_gather(amplitudes, 'row', axis=0, tiled=True), pr...  65.9 us
    scatter-add x1, other arithmetic, place_tiles(): return dense_block.at[position].add(tile_data, mode='drop')  61.8 us
    all_gather x1, waiting for transfers between devices, body(): lax.all_gather(amplitudes, 'row', axis=0, tiled=True)  56.5 us
    reshape x1, local copies, waits for them, and re-layouts, body(): dense_block.reshape(row_tiles, NV, TILE, TILE).transpose(0, 2, 1, 3)  53.5 us
    broadcast_in_dim x1, local copies, waits for them, and re-layouts, body(): empty_block = jnp.zeros((row_tiles * NV, TILE, TILE), jnp.bfloat16)  21.7 us
    unnamed x1, blocking collectives  18.5 us
  transfers between devices with their start and end apart: 2, of which 2 were waited for; matrix products, arithmetic and copies ran while one was open for 37% of the time, Pallas kernels for 0%

commit v1 on v0

--- a/solution.py
+++ b/solution.py
@@ -1,10 +1,16 @@
 import jax
 import jax.numpy as jnp
 from jax import lax
+from jax.experimental import pallas as pl
+from jax.experimental.pallas import tpu as pltpu
 from jax.sharding import PartitionSpec as P
 
 TILE = 128
 NV = 80
+MESH = pl.DeviceIdType.MESH
+CHUNK = 256
+GROUP = 5
+WIDE = 256
 
 
 def place_tiles(dense_block, pieces):
@@ -15,7 +21,7 @@
     return dense_block.at[position].add(tile_data, mode="drop")
 
 
-def body(amplitudes, integrals, tile_ab, tile_cd):
+def plain_body(amplitudes, integrals, tile_ab, tile_cd):
     row_tiles = amplitudes.shape[0] // TILE
     ab_code = tile_ab.astype(jnp.bfloat16)
     cd_code = tile_cd.astype(jnp.bfloat16)
@@ -41,6 +47,299 @@
     return result.astype(jnp.bfloat16)
 
 
+def ladder_kernel(
+    amp, ints, codes_in, out, a_all, v_all, codes, place, place_s, lhs, acc, stage,
+    own_sem, code_send, code_recv, xs, xr, ys, yr, fxs, fxr, fys, fyr,
+    up_s, down_s, line_r, sib_s, sib_r, out_sem,
+):
+    rows, width = amp.shape
+    slots = ints.shape[0]
+    chunks = rows // CHUNK
+    half = chunks // 2
+    row_tiles = rows // TILE
+    n_col = codes.shape[0]
+    n_z = n_col // 2
+    empty = n_col * slots
+
+    r = lax.axis_index("row")
+    c = lax.axis_index("col")
+    x, y = r % 2, r // 2
+    xn, yn, dg = r + 1 - 2 * x, r + 2 - 4 * y, 3 - r
+    z, core = c // 2, c % 2
+    sib = c + 1 - 2 * core
+
+    barrier = pltpu.get_barrier_semaphore()
+    for row in (xn, yn):
+        pl.semaphore_signal(barrier, inc=1, device_id=(row, c), device_id_type=MESH)
+    for d in range(1, n_col):
+        pl.semaphore_signal(barrier, inc=1, device_id=(r, (c + d) % n_col), device_id_type=MESH)
+    pl.semaphore_wait(barrier, n_col + 1)
+
+    def remote(src, dst, send, recv, device):
+        return pltpu.make_async_remote_copy(
+            src_ref=src, dst_ref=dst, send_sem=send, recv_sem=recv,
+            device_id=device, device_id_type=MESH,
+        )
+
+    def a_rows(block, j):
+        return a_all.at[pl.ds(pl.multiple_of(block * rows + j * CHUNK, CHUNK), CHUNK)]
+
+    def direct(j, owner, send, recv, device):
+        src = amp.at[pl.ds(j * CHUNK, CHUNK)]
+        return remote(src, a_rows(owner, j), send.at[j], recv.at[j], device)
+
+    def forward(j, s, owner, send, recv, device):
+        block = a_rows(owner, j)
+        return remote(block, block, send.at[s], recv.at[s], device)
+
+    def v_block(col):
+        return v_all.at[pl.ds(col * slots, slots)]
+
+    def own_v(send, recv, device):
+        return remote(ints, v_block(c), send, recv, device)
+
+    def pass_v(col, send, recv, device):
+        return remote(v_block(col), v_block(col), send, recv, device)
+
+    def code_copy(owner, peer):
+        return remote(codes_in, codes.at[owner], code_send.at[peer], code_recv.at[owner], (r, peer))
+
+    for d in range(1, n_col):
+        code_copy(c, (c + d) % n_col).start()
+    for i in range(half):
+        direct(i, r, xs, xr, (xn, c)).start()
+        direct(half + i, r, ys, yr, (yn, c)).start()
+
+    @pl.when(z < n_z - 1)
+    def _():
+        own_v(up_s.at[z], line_r.at[z], (r, c + 2)).start()
+
+    @pl.when(z > 0)
+    def _():
+        own_v(down_s.at[z], line_r.at[z], (r, c - 2)).start()
+
+    own_v(sib_s.at[z], sib_r.at[z], (r, sib)).start()
+    for i in range(half):
+        direct(half + i, r, xs, xr, (xn, c)).start()
+        direct(i, r, ys, yr, (yn, c)).start()
+
+    own_a = pltpu.make_async_copy(
+        amp, a_all.at[pl.ds(pl.multiple_of(r * rows, CHUNK), rows)], own_sem.at[0]
+    )
+    keep_v = pltpu.make_async_copy(ints, v_block(c), own_sem.at[1])
+    keep_code = pltpu.make_async_copy(codes_in, codes.at[c], own_sem.at[2])
+    own_a.start()
+    keep_v.start()
+    keep_code.start()
+    v_all[empty] = jnp.zeros((TILE, TILE), jnp.bfloat16)
+
+    keep_code.wait()
+    for d in range(1, n_col):
+        other = (c + d) % n_col
+        code_copy(other, other).wait_recv()
+    lane = lax.broadcasted_iota(jnp.int32, (slots, TILE), 1)
+    step = lax.broadcasted_iota(jnp.int32, (slots, TILE), 0)
+    for t in range(row_tiles):
+        found = jnp.full((slots, TILE), empty, jnp.int32)
+        for col in range(n_col):
+            hit = codes[col] == lane + t * TILE
+            found = jnp.minimum(found, jnp.where(hit, step + col * slots, empty))
+        place[t : t + 1, :] = jnp.min(found, axis=0, keepdims=True)
+    to_scalar = pltpu.make_async_copy(place, place_s, own_sem.at[3])
+    to_scalar.start()
+
+    def forward_a(i):
+        direct(i, xn, xs, xr, (xn, c)).wait_recv()
+        forward(i, i, xn, fys, fyr, (yn, c)).start()
+        direct(half + i, yn, ys, yr, (yn, c)).wait_recv()
+        forward(half + i, i, yn, fxs, fxr, (xn, c)).start()
+
+    def forward_v(d):
+        @pl.when(z >= d)
+        def _():
+            b = z - d
+            col = b * 2 + core
+            pass_v(col, up_s.at[b], line_r.at[b], (r, c)).wait_recv()
+
+            @pl.when(z < n_z - 1)
+            def _():
+                pass_v(col, up_s.at[b], line_r.at[b], (r, c + 2)).start()
+
+            pass_v(col, sib_s.at[b], sib_r.at[b], (r, sib)).start()
+
+        @pl.when(z + d < n_z)
+        def _():
+            b = z + d
+            col = b * 2 + core
+            pass_v(col, down_s.at[b], line_r.at[b], (r, c)).wait_recv()
+
+            @pl.when(z > 0)
+            def _():
+                pass_v(col, down_s.at[b], line_r.at[b], (r, c - 2)).start()
+
+            pass_v(col, sib_s.at[b], sib_r.at[b], (r, sib)).start()
+
+    for i in range(half):
+        forward_a(i)
+        if i == 2:
+            forward_v(1)
+        if i == 4:
+            forward_v(2)
+    forward_v(3)
+    keep_v.wait()
+    for b in range(n_z):
+        col = b * 2 + 1 - core
+        pass_v(col, sib_s.at[b], sib_r.at[b], (r, sib)).wait_recv()
+    to_scalar.wait()
+    own_a.wait()
+
+    def product(parts, first=False, last=False):
+        def group(g, carry):
+            top = pl.multiple_of(g * (GROUP * TILE), TILE)
+            spot = 0
+            for start, depth in parts:
+                for k in range(depth // TILE):
+                    tile_col = start // TILE + k
+                    for t in range(GROUP):
+                        lhs[t * TILE : (t + 1) * TILE, spot : spot + TILE] = v_all[
+                            place_s[g * GROUP + t, tile_col]
+                        ]
+                    spot += TILE
+            for n in range(0, width, WIDE):
+                total = None
+                spot = 0
+                for start, depth in parts:
+                    term = jnp.dot(
+                        lhs[:, spot : spot + depth],
+                        a_all[pl.ds(pl.multiple_of(start, CHUNK), depth), n : n + WIDE],
+                        preferred_element_type=jnp.float32,
+                    )
+                    total = term if total is None else total + term
+                    spot += depth
+                here = (pl.ds(top, GROUP * TILE), slice(n, n + WIDE))
+                if not first:
+                    total = total + acc[here]
+                if last:
+                    stage[here] = total.astype(jnp.bfloat16)
+                else:
+                    acc[here] = total
+            if last:
+                out_copy(g).start()
+            return carry
+
+        lax.fori_loop(0, row_tiles // GROUP, group, 0)
+
+    def out_copy(g):
+        span = pl.ds(pl.multiple_of(g * (GROUP * TILE), TILE), GROUP * TILE)
+        return pltpu.make_async_copy(stage.at[span], out.at[span], out_sem.at[g])
+
+    part = half * CHUNK
+    product([(r * rows, part)], first=True)
+    product([(r * rows + part, part)])
+    product([(xn * rows, part)])
+    product([(yn * rows + part, part)])
+
+    for i in range(half):
+        direct(half + i, xn, xs, xr, (xn, c)).wait_recv()
+    product([(xn * rows + part, part)])
+    for i in range(half):
+        direct(i, yn, ys, yr, (yn, c)).wait_recv()
+    product([(yn * rows, part)])
+
+    def diagonal(i, last):
+        forward(i, i, dg, fys, fyr, (yn, c)).wait_recv()
+        forward(half + i, i, dg, fxs, fxr, (xn, c)).wait_recv()
+        first = dg * rows + i * CHUNK
+        product([(first, CHUNK), (first + part, CHUNK)], last=last)
+
+    def diagonal_step(i, carry):
+        diagonal(i, False)
+        return carry
+
+    lax.fori_loop(0, half - 1, diagonal_step, 0)
+    diagonal(half - 1, True)
+
+    for d in range(1, n_col):
+        code_copy(c, (c + d) % n_col).wait_send()
+    for j in range(chunks):
+        direct(j, r, xs, xr, (xn, c)).wait_send()
+        direct(j, r, ys, yr, (yn, c)).wait_send()
+    for i in range(half):
+        forward(i, i, xn, fys, fyr, (yn, c)).wait_send()
+        forward(half + i, i, yn, fxs, fxr, (xn, c)).wait_send()
+    for b in range(n_z):
+        col = b * 2 + core
+
+        @pl.when((b <= z) & (z < n_z - 1))
+        def _():
+            pass_v(col, up_s.at[b], line_r.at[b], (r, c + 2)).wait_send()
+
+        @pl.when((b >= z) & (z > 0))
+        def _():
+            pass_v(col, down_s.at[b], line_r.at[b], (r, c - 2)).wait_send()
+
+        pass_v(col, sib_s.at[b], sib_r.at[b], (r, sib)).wait_send()
+    for g in range(row_tiles // GROUP):
+        out_copy(g).wait()
+
+
+def ladder_body(n_row, n_col):
+    def body(amplitudes, integrals, tile_ab, tile_cd):
+        rows, width = amplitudes.shape
+        slots = integrals.shape[0]
+        chunks = rows // CHUNK
+        half = chunks // 2
+        row_tiles = rows // TILE
+        code = jnp.where(tile_ab >= 0, tile_ab * TILE + tile_cd, -1)
+        code = jnp.broadcast_to(code[:, None], (slots, TILE))
+        dma = pltpu.SemaphoreType.DMA
+        place_rows = -(-row_tiles // 8) * 8
+        depth = n_row * rows
+        return pl.pallas_call(
+            ladder_kernel,
+            out_shape=jax.ShapeDtypeStruct((rows, width), jnp.bfloat16),
+            in_specs=[pl.BlockSpec(memory_space=pl.ANY)] * 3,
+            out_specs=pl.BlockSpec(memory_space=pl.ANY),
+            scratch_shapes=[
+                pltpu.VMEM((depth, width), jnp.bfloat16),
+                pltpu.VMEM((n_col * slots + 1, TILE, TILE), jnp.bfloat16),
+                pltpu.VMEM((n_col, slots, TILE), jnp.int32),
+                pltpu.VMEM((place_rows, TILE), jnp.int32),
+                pltpu.SMEM((place_rows, TILE), jnp.int32),
+                pltpu.VMEM((GROUP * TILE, half * CHUNK), jnp.bfloat16),
+                pltpu.VMEM((rows, width), jnp.float32),
+                pltpu.VMEM((rows, width), jnp.bfloat16),
+                dma((4,)),
+                dma((n_col,)),
+                dma((n_col,)),
+                dma((chunks,)),
+                dma((chunks,)),
+                dma((chunks,)),
+                dma((chunks,)),
+                dma((half,)),
+                dma((half,)),
+                dma((half,)),
+                dma((half,)),
+                dma((n_col // 2,)),
+                dma((n_col // 2,)),
+                dma((n_col // 2,)),
+                dma((n_col // 2,)),
+                dma((n_col // 2,)),
+                dma((row_tiles // GROUP,)),
+            ],
+            compiler_params=pltpu.CompilerParams(
+                collective_id=0, has_side_effects=True, vmem_limit_bytes=60 * 2**20
+            ),
+            cost_estimate=pl.CostEstimate(
+                flops=2 * rows * depth * width,
+                bytes_accessed=4 * rows * width,
+                transcendentals=0,
+            ),
+        )(amplitudes, integrals, code)
+
+    return body
+
+
 def solution(mesh):
     in_specs = (
         P("row", "col"),
@@ -49,4 +348,6 @@
         P(("row", "col")),
     )
     out_specs = P("row", "col")
+    n_row, n_col = mesh.shape["row"], mesh.shape["col"]
+    body = ladder_body(n_row, n_col) if (n_row, n_col) == (4, 8) else plain_body
     return jax.shard_map(body, mesh=mesh, in_specs=in_specs, out_specs=out_specs, check_vma=False)

time: 378 us -> 189 us (0.50)
  Pallas kernels: 0 us -> 182 us
  waiting for transfers between devices: 139 us -> 0 us
  local copies, waits for them, and re-layouts: 76.9 us -> 6.1 us
  matrix products: 65.9 us -> 0 us
  other arithmetic: 63.1 us -> 0.68 us
  blocking collectives: 18.5 us -> 0 us
  between operations: 14.1 us -> 0.01 us
    pallas_call x0 -> x1, Pallas kernels: none -> 182 us  [body(): pl.pallas_call(ladder_kernel, out_shape=jax.ShapeDtypeStruct((rows, width...]
    all_gather x2 -> x0, waiting for transfers between devices: 138 us -> none  [the longest x1 81 us: body(): lax.all_gather(integrals, 'col', axis=0, tiled=True)]
    dot_general x1 -> x0, matrix products: 65.9 us -> none  [body(): jnp.dot(matrix, lax.all_gather(amplitudes, 'row', axis=0, tiled=True), pr...]
    scatter-add x1 -> x0, other arithmetic: 61.8 us -> none  [place_tiles(): return dense_block.at[position].add(tile_data, mode='drop')]
    reshape x1 -> x0, local copies, waits for them, and re-layouts: 53.5 us -> none  [body(): dense_block.reshape(row_tiles, NV, TILE, TILE).transpose(0, 2, 1, 3)]
    broadcast_in_dim x1, local copies, waits for them, and re-layouts: 21.7 us -> 0.68 us  [body(): code = jnp.broadcast_to(code[:, None], (slots, TILE))]
    unnamed x1 -> x0, blocking collectives: 18.5 us -> none
  transfers between devices with their start and end apart: 2 -> 0, of which waited for: 2 -> 0; matrix products, arithmetic and copies ran while one was open for 37% -> 0% of each run, Pallas kernels for 0% -> 0%
where the time goes in v1:
time: 189 us
  Pallas kernels  182 us (96%)
  local copies, waits for them, and re-layouts  6.1 us (3%)
    pallas_call x1, Pallas kernels, body(): pl.pallas_call(ladder_kernel, out_shape=jax.ShapeDtypeStruct((rows, width...  182 us
    unnamed x1, local copies, waits for them, and re-layouts  5.42 us

profile of v1, /device:TPU:0, one launch (start us, length us, event | category | flops | bytes accessed | tf_op | source)
XLA Modules:
  0.0 188.6 jit_solution(2138178516421935513)
XLA Ops:
  0.0 0.7 compare_select_fusion
  0.7 0.7 broadcast_in_dim.11.codes_in
  1.4 181.8 %shard_map.46 = bf16[2560,1024]{1,0:T(8,128)(2,1)} custom-call(bf16[2560,1024]{1,0:T(8,128)(2,1)} %amp.1, bf16[40,128,128]{2,1,0:T(8,128)(2,1)} %ints.1, s32[40,128]{1,0:T(8,128)} %broadcast_in_dim.11.codes_in), custom_call_target="tpu_custom_call" | custom-call | flops 53687091200 | bytes 10485760 | tf_op jit(solution)/shard_map/pallas_call | solution.py:298
  183.2 5.4 %copy.6 = bf16[2560,1024]{1,0:T(8,128)(2,1)} copy(bf16[2560,1024]{1,0:T(8,128)(2,1)} %shard_map.46) | data formatting | bytes 10485760

commit v2 on v1

--- a/solution.py
+++ b/solution.py
@@ -48,9 +48,9 @@
 
 
 def ladder_kernel(
-    amp, ints, codes_in, out, a_all, v_all, codes, place, place_s, lhs, acc, stage,
+    amp, ints, tile_ab, tile_cd, out, a_all, v_all, codes_in, codes, place, place_s, lhs, acc,
     own_sem, code_send, code_recv, xs, xr, ys, yr, fxs, fxr, fys, fyr,
-    up_s, down_s, line_r, sib_s, sib_r, out_sem,
+    up_s, down_s, line_r, sib_s, sib_r,
 ):
     rows, width = amp.shape
     slots = ints.shape[0]
@@ -104,8 +104,6 @@
     def code_copy(owner, peer):
         return remote(codes_in, codes.at[owner], code_send.at[peer], code_recv.at[owner], (r, peer))
 
-    for d in range(1, n_col):
-        code_copy(c, (c + d) % n_col).start()
     for i in range(half):
         direct(i, r, xs, xr, (xn, c)).start()
         direct(half + i, r, ys, yr, (yn, c)).start()
@@ -119,6 +117,11 @@
         own_v(down_s.at[z], line_r.at[z], (r, c - 2)).start()
 
     own_v(sib_s.at[z], sib_r.at[z], (r, sib)).start()
+    for s in range(slots):
+        code = tile_ab[s] * TILE + tile_cd[s]
+        codes_in[s : s + 1, :] = jnp.full((1, TILE), code, jnp.int32)
+    for d in range(1, n_col):
+        code_copy(c, (c + d) % n_col).start()
     for i in range(half):
         direct(half + i, r, xs, xr, (xn, c)).start()
         direct(i, r, ys, yr, (yn, c)).start()
@@ -220,18 +223,12 @@
                 if not first:
                     total = total + acc[here]
                 if last:
-                    stage[here] = total.astype(jnp.bfloat16)
+                    out[here] = total.astype(jnp.bfloat16)
                 else:
                     acc[here] = total
-            if last:
-                out_copy(g).start()
             return carry
 
         lax.fori_loop(0, row_tiles // GROUP, group, 0)
-
-    def out_copy(g):
-        span = pl.ds(pl.multiple_of(g * (GROUP * TILE), TILE), GROUP * TILE)
-        return pltpu.make_async_copy(stage.at[span], out.at[span], out_sem.at[g])
 
     part = half * CHUNK
     product([(r * rows, part)], first=True)
@@ -279,8 +276,6 @@
             pass_v(col, down_s.at[b], line_r.at[b], (r, c - 2)).wait_send()
 
         pass_v(col, sib_s.at[b], sib_r.at[b], (r, sib)).wait_send()
-    for g in range(row_tiles // GROUP):
-        out_copy(g).wait()
 
 
 def ladder_body(n_row, n_col):
@@ -290,25 +285,23 @@
         chunks = rows // CHUNK
         half = chunks // 2
         row_tiles = rows // TILE
-        code = jnp.where(tile_ab >= 0, tile_ab * TILE + tile_cd, -1)
-        code = jnp.broadcast_to(code[:, None], (slots, TILE))
         dma = pltpu.SemaphoreType.DMA
         place_rows = -(-row_tiles // 8) * 8
         depth = n_row * rows
         return pl.pallas_call(
             ladder_kernel,
-            out_shape=jax.ShapeDtypeStruct((rows, width), jnp.bfloat16),
-            in_specs=[pl.BlockSpec(memory_space=pl.ANY)] * 3,
-            out_specs=pl.BlockSpec(memory_space=pl.ANY),
+            out_shape=pltpu.VMEM((rows, width), jnp.bfloat16),
+            in_specs=[pl.BlockSpec(memory_space=pl.ANY)] * 2 + [pl.BlockSpec(memory_space=pltpu.SMEM)] * 2,
+            out_specs=pl.BlockSpec(memory_space=pltpu.VMEM),
             scratch_shapes=[
                 pltpu.VMEM((depth, width), jnp.bfloat16),
                 pltpu.VMEM((n_col * slots + 1, TILE, TILE), jnp.bfloat16),
+                pltpu.VMEM((slots, TILE), jnp.int32),
                 pltpu.VMEM((n_col, slots, TILE), jnp.int32),
                 pltpu.VMEM((place_rows, TILE), jnp.int32),
                 pltpu.SMEM((place_rows, TILE), jnp.int32),
                 pltpu.VMEM((GROUP * TILE, half * CHUNK), jnp.bfloat16),
                 pltpu.VMEM((rows, width), jnp.float32),
-                pltpu.VMEM((rows, width), jnp.bfloat16),
                 dma((4,)),
                 dma((n_col,)),
                 dma((n_col,)),
@@ -325,17 +318,16 @@
                 dma((n_col // 2,)),
                 dma((n_col // 2,)),
                 dma((n_col // 2,)),
-                dma((row_tiles // GROUP,)),
             ],
             compiler_params=pltpu.CompilerParams(
-                collective_id=0, has_side_effects=True, vmem_limit_bytes=60 * 2**20
+                collective_id=0, has_side_effects=True, vmem_limit_bytes=50 * 2**20
             ),
             cost_estimate=pl.CostEstimate(
                 flops=2 * rows * depth * width,
                 bytes_accessed=4 * rows * width,
                 transcendentals=0,
             ),
-        )(amplitudes, integrals, code)
+        )(amplitudes, integrals, tile_ab, tile_cd)
 
     return body
 

time: 189 us -> 184 us (0.974)
  local copies, waits for them, and re-layouts: 6.1 us -> 2.36 us
    unnamed x1, local copies, waits for them, and re-layouts: 5.42 us -> 2.36 us
where the time goes in v2:
time: 184 us
  Pallas kernels  181 us (98%)
  local copies, waits for them, and re-layouts  2.36 us (1%)
    pallas_call x1, Pallas kernels, body(): pl.pallas_call(ladder_kernel, out_shape=pltpu.VMEM((rows, width), jnp.bfl...  181 us

profile of v2, /device:TPU:0, one launch (start us, length us, event | category | flops | bytes accessed | tf_op | source)
XLA Modules:
  0.0 183.8 jit_solution(5452999749092623882)
XLA Ops:
  0.0 181.4 %shard_map.46 = bf16[2560,1024]{1,0:T(8,128)(2,1)S(1)} custom-call(bf16[2560,1024]{1,0:T(8,128)(2,1)} %amp.1, bf16[40,128,128]{2,1,0:T(8,128)(2,1)} %ints.1, s32[40]{0:T(128)} %tile_ab.1, s32[40]{0:T(128)} %tile_cd.1), custom_call_target="tpu_custom_call" | custom-call | flops 53687091200 | bytes 10485760 | tf_op jit(solution)/shard_map/pallas_call | solution.py:291
  181.5 2.4 %copy.6 = bf16[2560,1024]{1,0:T(8,128)(2,1)} copy(bf16[2560,1024]{1,0:T(8,128)(2,1)S(1)} %shard_map.46) | data formatting | bytes 10485760

commit v3 on v2

--- a/solution.py
+++ b/solution.py
@@ -243,18 +243,19 @@
         direct(i, yn, ys, yr, (yn, c)).wait_recv()
     product([(yn * rows, part)])
 
-    def diagonal(i, last):
+    def diagonal_step(i, carry):
         forward(i, i, dg, fys, fyr, (yn, c)).wait_recv()
         forward(half + i, i, dg, fxs, fxr, (xn, c)).wait_recv()
         first = dg * rows + i * CHUNK
-        product([(first, CHUNK), (first + part, CHUNK)], last=last)
-
-    def diagonal_step(i, carry):
-        diagonal(i, False)
+        product([(first, CHUNK), (first + part, CHUNK)])
         return carry
 
     lax.fori_loop(0, half - 1, diagonal_step, 0)
-    diagonal(half - 1, True)
+    end = half - 1
+    forward(end, end, dg, fys, fyr, (yn, c)).wait_recv()
+    product([(dg * rows + end * CHUNK, CHUNK)])
+    forward(half + end, end, dg, fxs, fxr, (xn, c)).wait_recv()
+    product([(dg * rows + part + end * CHUNK, CHUNK)], last=True)
 
     for d in range(1, n_col):
         code_copy(c, (c + d) % n_col).wait_send()

time: 184 us -> 185 us (level)
  no operation moved by 1% of the time
where the time goes in v3:
time: 185 us
  Pallas kernels  182 us (98%)
  local copies, waits for them, and re-layouts  2.36 us (1%)
    pallas_call x1, Pallas kernels, body(): pl.pallas_call(ladder_kernel, out_shape=pltpu.VMEM((rows, width), jnp.bfl...  182 us

profile of v3, /device:TPU:0, one launch (start us, length us, event | category | flops | bytes accessed | tf_op | source)
XLA Modules:
  0.0 184.5 jit_solution(13162957260305124581)
XLA Ops:
  0.0 182.1 %shard_map.46 = bf16[2560,1024]{1,0:T(8,128)(2,1)S(1)} custom-call(bf16[2560,1024]{1,0:T(8,128)(2,1)} %amp.1, bf16[40,128,128]{2,1,0:T(8,128)(2,1)} %ints.1, s32[40]{0:T(128)} %tile_ab.1, s32[40]{0:T(128)} %tile_cd.1), custom_call_target="tpu_custom_call" | custom-call | flops 53687091200 | bytes 10485760 | tf_op jit(solution)/shard_map/pallas_call | solution.py:292
  182.1 2.4 %copy.6 = bf16[2560,1024]{1,0:T(8,128)(2,1)} copy(bf16[2560,1024]{1,0:T(8,128)(2,1)S(1)} %shard_map.46) | data formatting | bytes 10485760

commit v4 on v2

--- a/solution.py
+++ b/solution.py
@@ -48,7 +48,7 @@
 
 
 def ladder_kernel(
-    amp, ints, tile_ab, tile_cd, out, a_all, v_all, codes_in, codes, place, place_s, lhs, acc,
+    amp, ints, tile_ab, tile_cd, out, a_all, v_all, codes_in, codes, place, place_s, lhs, lhs_end, acc,
     own_sem, code_send, code_recv, xs, xr, ys, yr, fxs, fxr, fys, fyr,
     up_s, down_s, line_r, sib_s, sib_r,
 ):
@@ -196,11 +196,14 @@
     to_scalar.wait()
     own_a.wait()
 
+    def left(top, last):
+        return lhs_end.at[pl.ds(top, GROUP * TILE)] if last else lhs
+
     def product(parts, first=False, last=False):
         def group(g, carry):
             top = pl.multiple_of(g * (GROUP * TILE), TILE)
             spot = 0
-            for start, depth in parts:
+            for start, depth in [] if last else parts:
                 for k in range(depth // TILE):
                     tile_col = start // TILE + k
                     for t in range(GROUP):
@@ -213,7 +216,7 @@
                 spot = 0
                 for start, depth in parts:
                     term = jnp.dot(
-                        lhs[:, spot : spot + depth],
+                        left(top, last)[:, spot : spot + depth],
                         a_all[pl.ds(pl.multiple_of(start, CHUNK), depth), n : n + WIDE],
                         preferred_element_type=jnp.float32,
                     )
@@ -253,6 +256,16 @@
         diagonal(i, False)
         return carry
 
+    end = (dg * rows + (half - 1) * CHUNK) // TILE
+
+    def read_end(t, carry):
+        for k in range(2 * CHUNK // TILE):
+            tile_col = end + k if k < CHUNK // TILE else end + part // TILE + k - CHUNK // TILE
+            span = pl.ds(pl.multiple_of(t * TILE, TILE), TILE)
+            lhs_end[span, k * TILE : (k + 1) * TILE] = v_all[place_s[t, tile_col]]
+        return carry
+
+    lax.fori_loop(0, row_tiles, read_end, 0)
     lax.fori_loop(0, half - 1, diagonal_step, 0)
     diagonal(half - 1, True)
 
@@ -301,6 +314,7 @@
                 pltpu.VMEM((place_rows, TILE), jnp.int32),
                 pltpu.SMEM((place_rows, TILE), jnp.int32),
                 pltpu.VMEM((GROUP * TILE, half * CHUNK), jnp.bfloat16),
+                pltpu.VMEM((rows, 2 * CHUNK), jnp.bfloat16),
                 pltpu.VMEM((rows, width), jnp.float32),
                 dma((4,)),
                 dma((n_col,)),

time: 184 us -> 184 us (level)
  no operation moved by 1% of the time
where the time goes in v4:
time: 184 us
  Pallas kernels  181 us (98%)
  local copies, waits for them, and re-layouts  2.36 us (1%)
    pallas_call x1, Pallas kernels, body(): pl.pallas_call(ladder_kernel, out_shape=pltpu.VMEM((rows, width), jnp.bfl...  181 us

profile of v4, /device:TPU:0, one launch (start us, length us, event | category | flops | bytes accessed | tf_op | source)
XLA Modules:
  0.0 183.8 jit_solution(7512519835165696092)
XLA Ops:
  0.0 181.4 %shard_map.46 = bf16[2560,1024]{1,0:T(8,128)(2,1)S(1)} custom-call(bf16[2560,1024]{1,0:T(8,128)(2,1)} %amp.1, bf16[40,128,128]{2,1,0:T(8,128)(2,1)} %ints.1, s32[40]{0:T(128)} %tile_ab.1, s32[40]{0:T(128)} %tile_cd.1), custom_call_target="tpu_custom_call" | custom-call | flops 53687091200 | bytes 10485760 | tf_op jit(solution)/shard_map/pallas_call | solution.py:304
  181.4 2.4 %copy.6 = bf16[2560,1024]{1,0:T(8,128)(2,1)} copy(bf16[2560,1024]{1,0:T(8,128)(2,1)S(1)} %shard_map.46) | data formatting | bytes 10485760
